TPU v7x, 32 devices: a whole 2x2x4 slice. The times are simulated.
32 devices in a mesh: blk: 4 (over y, x), rep: 8 (over z, core).
Axes of the slice: x: 2, y: 2, z: 4, core: 2. Of those that a mesh axis runs over, the one named last changes fastest.
Arguments:
- node_feats: bfloat16 [12288, 128], P(('blk', 'rep')), may hold values from -6 to 6
- block_vals: bfloat16 [4, 8, 4, 40, 128, 128], P('blk', 'rep'), may hold values from 0.00049972534 to 0.049804688
- block_rows: int32 [4, 8, 4, 40], P('blk', 'rep'), may hold values from 0 to 23
- block_cols: int32 [4, 8, 4, 40], P('blk', 'rep'), may hold values from 0 to 2
- block_count: int32 [4, 8, 4], P('blk', 'rep'), may hold values from 1 to 40, as said below
- weight: bfloat16 [128, 256], replicated, may hold values from -0.5 to 0.5
Outputs:
- layer_out: bfloat16 [12288, 256], P(('blk', 'rep'))
Inputs may be any that keep to these rules, and one draw needn't show every extreme that they name: Only the first block_count[b, r, j] slots of list (b, r, j) are live; the values, rows and columns of later slots are ignored. The largest count 40 is reached in every draw.
All inputs are finite; a program needn't handle non-finite values.
Results may differ from a plain program's by a relative error of at most 0.0011.
Values may be sent and summed in bfloat16 or wider, within the bound.
A program may use at most 128 MiB of HBM per device.

v0:
```python
import jax
import jax.numpy as jnp
from jax import lax
from jax.sharding import PartitionSpec as P

BS = 128
PIECE_BLK = 3


def shifted(array, axis, by):
    size = lax.axis_size(axis)
    return lax.ppermute(array, axis, [(i, (i + by) % size) for i in range(size)])


def add_blocks(panel_sum, x_piece, blk_vals, row_ids, col_ids, live_count):
    piece_count = x_piece.shape[0]
    panel_count = panel_sum.shape[0]
    col_select = (col_ids[:, None] == jnp.arange(piece_count, dtype=jnp.int32)[None, :]).astype(
        jnp.bfloat16
    )
    gathered = jnp.einsum(
        "sk,kbf->sbf", col_select, x_piece, preferred_element_type=jnp.float32
    ).astype(jnp.bfloat16)
    products = jnp.einsum("sab,sbf->saf", blk_vals, gathered, preferred_element_type=jnp.float32)
    in_use = jnp.arange(row_ids.shape[0], dtype=jnp.int32) < live_count
    row_select = jnp.logical_and(
        row_ids[:, None] == jnp.arange(panel_count, dtype=jnp.int32)[None, :], in_use[:, None]
    )
    row_select = row_select.astype(jnp.float32)
    added = jnp.einsum(
        "sk,saf->kaf",
        row_select,
        products,
        precision=lax.Precision.HIGHEST,
        preferred_element_type=jnp.float32,
    )
    return panel_sum + added


def absorb(panel_sum, x_piece, list_vals, list_rows, list_cols, list_count, source):
    blk_vals = lax.dynamic_index_in_dim(list_vals, source, 0, keepdims=False)
    row_ids = lax.dynamic_index_in_dim(list_rows, source, 0, keepdims=False)
    col_ids = lax.dynamic_index_in_dim(list_cols, source, 0, keepdims=False)
    live_count = lax.dynamic_index_in_dim(list_count, source, 0, keepdims=False)
    return add_blocks(panel_sum, x_piece, blk_vals, row_ids, col_ids, live_count)


def local(node_feats, block_vals, block_rows, block_cols, block_count, weight):
    cycle_size = lax.axis_size("blk")
    position = lax.axis_index("blk")
    feat_width = node_feats.shape[1]
    x_piece = node_feats.reshape(-1, BS, feat_width)
    list_vals = block_vals[0, 0]
    list_rows = block_rows[0, 0]
    list_cols = block_cols[0, 0]
    list_count = block_count[0, 0]
    panel_blocks = PIECE_BLK * lax.axis_size("rep")
    panel_sum = jnp.zeros((panel_blocks, BS, feat_width), jnp.float32)
    panel_sum = absorb(
        panel_sum, x_piece, list_vals, list_rows, list_cols, list_count, position % cycle_size
    )
    held = x_piece
    for section in range(1, cycle_size):
        held = shifted(held, "blk", 1)
        source = (position - section) % cycle_size
        panel_sum = absorb(panel_sum, held, list_vals, list_rows, list_cols, list_count, source)
    flat_panel = panel_sum.reshape(-1, feat_width)
    weight_full = weight.astype(jnp.float32)
    agg_rows = lax.psum_scatter(flat_panel, "rep", scatter_dimension=0, tiled=True)
    result = jnp.dot(agg_rows, weight_full, precision=lax.Precision.HIGHEST)
    return jnp.maximum(result, 0.0).astype(jnp.bfloat16)


def solution(mesh):
    return jax.shard_map(
        local,
        mesh=mesh,
        in_specs=(
            P(("blk", "rep"), None),
            P("blk", "rep", None, None, None, None),
            P("blk", "rep", None, None),
            P("blk", "rep", None, None),
            P("blk", "rep", None),
            P(),
        ),
        out_specs=P(("blk", "rep"), None),
        check_vma=False,
    )
```

profile of v0, /device:TPU:0, one launch (start us, length us, event | category | flops | bytes accessed | tf_op | source)
XLA Modules:
  0.0 82.8 jit_solution(15558128347192679538)
XLA Ops:
  6.5 2.9 %collective-permute-start = (bf16[3,128,128]{2,1,0:T(8,128)(2,1)}, bf16[3,128,128]{2,1,0:T(8,128)(2,1)S(1)}, u32[]{:S(2)}, u32[]{:S(2)}) collective-permute-start(bf16[3,128,128]{2,1,0:T(8,128)(2,1)} %bitcast.61), channel_id=1, source_target_pairs={{0,8},{8,16},{16,24},{24,0},{1,9},{9,17},{17,25},{25,1},{2,10},{10... | collective-permute-start | bytes 294920 | tf_op jit(solution)/shard_map/ppermute | solution.py:12
  9.5 1.5 %constant_dynamic-slice_fusion.10 = (s32[1,1,1]{2,1,0:T(1,128)}, s32[1,1,1]{2,1,0:T(1,128)}, s32[1,1,1]{2,1,0:T(1,128)}, s32[1,1,1]{2,1,0:T(1,128)}) fusion(s32[1,1,4]{2,1,0:T(1,128)} %param.10, s32[]{:T(128)S(6)} %select_n.47, s32[]{:T(128)S(6)} %select_n.49, s32[]{:T(128)S(6)} %select_n.53, s32[]{:T(128)S(6)} %select_n.51), kind=kLoop, calls=%fused_computation.81 | loop fusion | bytes 48 | tf_op jit(solution)/shard_map/jit(dynamic_index_in_dim)/dynamic_slice | solution.py:44
  10.9 0.6 iota_compare_fusion.11
  11.6 0.6 iota_compare_fusion.10
  12.2 0.7 iota_compare_fusion.8
  12.9 0.9 %fusion.67 = (s32[40]{0:T(128)S(1)}, s32[40]{0:T(128)S(1)}, s32[40]{0:T(128)S(1)}, s32[40]{0:T(128)S(1)}, s32[40]{0:T(128)S(1)}, /*index=5*/s32[40]{0:T(128)S(1)}, s32[40]{0:T(128)S(1)}, s32[40]{0:T(128)S(1)}) fusion(s32[1,1,4,40]{3,2,1,0:T(4,128)} %param.8, s32[]{:T(128)S(6)} %select_n.47, s32[]{:T(128)S(6)} %select_n.49, s32[]{:T(128)S(6)} %select_n.53, ...), kind=kLoop, calls=%fused_computation.83 | loop fusion | bytes 2576 | tf_op jit(solution)/shard_map/eq | solution.py:27
  13.7 1.4 %fusion.29 = bf16[40,128,128]{2,0,1:T(8,128)(2,1)S(1)} fusion(bf16[3,128,128]{2,1,0:T(8,128)(2,1)} %bitcast.62, s32[40]{0:T(128)S(1)} %get-tuple-element.20), kind=kOutput, calls=%fused_computation.33 | convolution fusion | flops 3932280 | bytes 1409184 | tf_op jit(solution)/shard_map/sk,kbf->sbf/dot_general | solution.py:21
  15.2 2.0 %fusion.10 = f32[40,128,128]{2,1,0:T(8,128)S(1)} fusion(bf16[40,128,128]{2,0,1:T(8,128)(2,1)S(1)} %fusion.29, bf16[1,1,4,40,128,128]{5,4,3,2,1,0:T(8,128)(2,1)} %param.7, s32[]{:T(128)S(6)} %select_n.47), kind=kOutput, calls=%fused_computation.13 | convolution fusion | flops 167772160 | bytes 5242884 | tf_op jit(solution)/shard_map/sab,sbf->saf/dot_general | solution.py:24
  17.1 0.6 iota_compare_fusion.9
  17.8 0.5 fusion.27
  18.9 1.6 %collective-permute-start.1 = (bf16[3,128,128]{2,1,0:T(8,128)(2,1)S(1)}, bf16[3,128,128]{2,1,0:T(8,128)(2,1)S(1)}, u32[]{:S(2)}, u32[]{:S(2)}) collective-permute-start(bf16[3,128,128]{2,1,0:T(8,128)(2,1)S(1)} %collective-permute-done), channel_id=1, source_target_pairs={{0,8},{8,16},{16,24},{24,0},{1,9},{9,17},{17,25},{25,1},{2,10},{10... | collective-permute-start | bytes 294920 | tf_op jit(solution)/shard_map/ppermute | solution.py:12
  20.4 2.6 %fusion.4 = f32[24,128,128]{2,0,1:T(8,128)S(1)} fusion(f32[40,128,128]{2,1,0:T(8,128)S(1)} %fusion.11, s32[40]{0:T(128)S(1)} %get-tuple-element.6, pred[40]{0:T(512)(128)(4,1)S(1)} %iota_compare_fusion.10), kind=kOutput, calls=%fused_computation.6 | convolution fusion | flops 188745600 | bytes 4194504 | tf_op jit(solution)/shard_map/sk,saf->kaf/dot_general | solution.py:30
  23.0 1.4 %collective-permute-done.1 = bf16[3,128,128]{2,1,0:T(8,128)(2,1)S(1)} collective-permute-done((bf16[3,128,128]{2,1,0:T(8,128)(2,1)S(1)}, bf16[3,128,128]{2,1,0:T(8,128)(2,1)S(1)}, u32[]{:S(2)}, u32[]{:S(2)}) %collective-permute-start.1) | collective-permute-done | bytes 98336 | tf_op jit(solution)/shard_map/ppermute | solution.py:12
  24.4 0.5 fusion.25
  25.5 0.8 collective-permute-start.2
  26.3 2.6 %fusion.2 = f32[24,128,128]{2,0,1:T(8,128)S(1)} fusion(f32[40,128,128]{2,1,0:T(8,128)S(1)} %fusion.12, s32[40]{0:T(128)S(1)} %get-tuple-element.8, pred[40]{0:T(512)(128)(4,1)S(1)} %iota_compare_fusion.9), kind=kOutput, calls=%fused_computation.3 | convolution fusion | flops 188745600 | bytes 4194504 | tf_op jit(solution)/shard_map/sk,saf->kaf/dot_general | solution.py:30
  28.9 2.4 %collective-permute-done.2 = bf16[3,128,128]{2,1,0:T(8,128)(2,1)S(1)} collective-permute-done((bf16[3,128,128]{2,1,0:T(8,128)(2,1)S(1)}, bf16[3,128,128]{2,1,0:T(8,128)(2,1)S(1)}, u32[]{:S(2)}, u32[]{:S(2)}) %collective-permute-start.2) | collective-permute-done | bytes 98336 | tf_op jit(solution)/shard_map/ppermute | solution.py:12
  31.2 0.5 fusion.23
  31.8 0.5 fusion.13
  32.3 2.6 %fusion = f32[24,128,128]{2,0,1:T(8,128)S(1)} fusion(f32[40,128,128]{2,1,0:T(8,128)S(1)} %fusion.13, s32[40]{0:T(128)S(1)} %get-tuple-element.7, pred[40]{0:T(512)(128)(4,1)S(1)} %iota_compare_fusion.8), kind=kOutput, calls=%fused_computation | convolution fusion | flops 188745600 | bytes 4194504 | tf_op jit(solution)/shard_map/sk,saf->kaf/dot_general | solution.py:30
  34.9 2.9 %add_add_fusion = f32[24,128,128]{2,0,1:T(8,128)S(1)} fusion(f32[24,128,128]{2,0,1:T(8,128)S(1)} %fusion, f32[24,128,128]{2,0,1:T(8,128)S(1)} %fusion.2, f32[24,128,128]{2,0,1:T(8,128)S(1)} %fusion.4, f32[40,128,128]{2,1,0:T(8,128)S(1)} %fusion.10, s32[40]{0:T(128)S(1)} %get-tuple-element.5, pred[40]{0:T(512)(128)(4,1)S(1)} %iota_compare_fusion.11), kind=kOutput, calls=%fused_computation.12 | convolution fusion | flops 189925248 | bytes 8913096 | tf_op jit(solution)/shard_map/sk,saf->kaf/dot_general | solution.py:30
  37.8 1.4 %copy.7 = f32[24,128,128]{2,1,0:T(8,128)} copy(f32[24,128,128]{2,0,1:T(8,128)S(1)} %add_add_fusion) | data formatting | bytes 3145728 | tf_op jit(solution)/shard_map/add | solution.py:37
  39.3 34.8 %reduce-scatter.2.cloned.1.call-done = f32[384,128]{1,0:T(8,128)} async-done(((f32[3072,128]{1,0:T(8,128)}), f32[384,128]{1,0:T(8,128)}) %reduce-scatter.2.cloned.1.call-update) | async-done | bytes 196624 | tf_op jit(solution)/shard_map/reduce_scatter | solution.py:69
  74.0 1.9 %fusion.22 = bf16[384,256]{1,0:T(8,128)(2,1)} fusion(f32[384,128]{1,0:T(8,128)} %reduce-scatter.2.cloned.1.call-done, bf16[128,256]{1,0:T(8,128)(2,1)S(1)} %copy-done), kind=kOutput, calls=%fused_computation.26 | convolution fusion | flops 151191552 | bytes 458752 | tf_op jit(solution)/shard_map/dot_general | solution.py:70
  (9 shorter events, 1.0 us)
Async XLA Ops:
  6.5 67.5 %copy-start = (bf16[128,256]{1,0:T(8,128)(2,1)S(1)}, bf16[128,256]{1,0:T(8,128)(2,1)}, u32[]{:S(2)}) copy-start(bf16[128,256]{1,0:T(8,128)(2,1)} %param.11) | copy-start | bytes 196612
  6.5 67.5 %reduce-scatter.2.cloned.1.call-start = ((), (), s32[]{:S(2)}) async-start(), calls=%async_computation.1 | async-start | bytes 1769472 | tf_op jit(solution)/shard_map/reduce_scatter | solution.py:69
  6.5 11.2 %collective-permute-start = (bf16[3,128,128]{2,1,0:T(8,128)(2,1)}, bf16[3,128,128]{2,1,0:T(8,128)(2,1)S(1)}, u32[]{:S(2)}, u32[]{:S(2)}) collective-permute-start(bf16[3,128,128]{2,1,0:T(8,128)(2,1)} %bitcast.61), channel_id=1, source_target_pairs={{0,8},{8,16},{16,24},{24,0},{1,9},{9,17},{17,25},{25,1},{2,10},{10... | collective-permute-start | bytes 294920 | tf_op jit(solution)/shard_map/ppermute | solution.py:12
  15.2 3.2 %copy-start.1 = (bf16[1,1,4,40,128,128]{5,4,3,2,1,0:T(8,128)(2,1)S(1)}, bf16[1,1,4,40,128,128]{5,4,3,2,1,0:T(8,128)(2,1)}, u32[]{:S(2)}) copy-start(bf16[1,1,4,40,128,128]{5,4,3,2,1,0:T(8,128)(2,1)} %param.7) | copy-start | bytes 15728644
  18.9 5.6 %collective-permute-start.1 = (bf16[3,128,128]{2,1,0:T(8,128)(2,1)S(1)}, bf16[3,128,128]{2,1,0:T(8,128)(2,1)S(1)}, u32[]{:S(2)}, u32[]{:S(2)}) collective-permute-start(bf16[3,128,128]{2,1,0:T(8,128)(2,1)S(1)} %collective-permute-done), channel_id=1, source_target_pairs={{0,8},{8,16},{16,24},{24,0},{1,9},{9,17},{17,25},{25,1},{2,10},{10... | collective-permute-start | bytes 294920 | tf_op jit(solution)/shard_map/ppermute | solution.py:12
  25.5 5.7 %collective-permute-start.2 = (bf16[3,128,128]{2,1,0:T(8,128)(2,1)S(1)}, bf16[3,128,128]{2,1,0:T(8,128)(2,1)S(1)}, u32[]{:S(2)}, u32[]{:S(2)}) collective-permute-start(bf16[3,128,128]{2,1,0:T(8,128)(2,1)S(1)} %collective-permute-done.1), channel_id=1, source_target_pairs={{0,8},{8,16},{16,24},{24,0},{1,9},{9,17},{17,25},{25,1},{2,10},{10... | collective-permute-start | bytes 294920 | tf_op jit(solution)/shard_map/ppermute | solution.py:12
Sparse Core Ops, SparseCore 0:
  39.4 34.5 reduce-scatter.1
where the time goes:
time: 83 us; the launch traced here: 82.8 us
  waiting for transfers between devices  38.6 us (47%)
  matrix products  19.1 us (23%)
  between operations  13.5 us (16%)
  starting transfers between devices  5.32 us (6%)
  local copies, waits for them, and re-layouts  3.75 us (5%)
  other arithmetic  2.53 us (3%)
    reduce_scatter x1, waiting for transfers between devices, local(): lax.psum_scatter(flat_panel, 'rep', scatter_dimension=0, tiled=True)  34.8 us
    dot_general x4, matrix products, add_blocks(): jnp.einsum('sk,saf->kaf', row_select, products, precision=lax.Precision.H...  10.6 us
    ppermute x3, starting transfers between devices, shifted(): lax.ppermute(array, axis, [(i, (i + by) % size) for i in range(size)])  5.31 us
    ppermute x3, waiting for transfers between devices, shifted(): lax.ppermute(array, axis, [(i, (i + by) % size) for i in range(size)])  3.8 us
    dot_general x4, matrix products, add_blocks(): jnp.einsum('sab,sbf->saf', blk_vals, gathered, preferred_element_type=jnp...  3.49 us
    dot_general x4, matrix products, add_blocks(): jnp.einsum('sk,kbf->sbf', col_select, x_piece, preferred_element_type=jnp...  3.07 us
    lt x4, other arithmetic, add_blocks(): in_use = jnp.arange(row_ids.shape[0], dtype=jnp.int32) < live_count  2.53 us
    dot_general x1, matrix products, local(): result = jnp.dot(agg_rows, weight_full, precision=lax.Precision.HIGHEST)  1.92 us
  transfers between devices with their start and end apart: 4, of which 3 were waited for; matrix products, arithmetic and copies ran while one was open for 16% of the time, Pallas kernels for 0%

commit v1 on v0

v1 whole, which is shorter than its diff:
```python
import functools

import jax
import jax.numpy as jnp
from jax import lax
from jax.experimental import pallas as pl
from jax.experimental.pallas import tpu as pltpu
from jax.sharding import PartitionSpec as P

BS = 128
LEVELS = 32000.0
STEPS = 256.0
TINY = 1e-36
PAD = 16
MESH = pl.DeviceIdType.MESH


def flip(index, mask, size):
    if size & (size - 1):
        return (index + mask) % size
    out = index
    bit = 1
    while bit < size:
        if mask & bit:
            out = out + bit * (1 - 2 * ((index // bit) % 2))
        bit *= 2
    return out


def back(mask, size):
    return (size - mask) % size if size & (size - 1) else mask


def pack(total, box):
    rows = total.shape[0]
    top = jnp.max(jnp.abs(total), axis=0, keepdims=True)
    code = jnp.ceil(jnp.log2(jnp.maximum(top, TINY)) * STEPS)
    inverse = 1.0 / jnp.exp2(code * (1.0 / STEPS))
    scaled = jnp.round(total * inverse * LEVELS)
    box[pl.ds(0, rows)] = scaled.astype(jnp.int32).astype(jnp.int16)
    box[pl.ds(rows, PAD)] = (
        jnp.broadcast_to(code, (PAD, code.shape[1])).astype(jnp.int32).astype(jnp.int16)
    )


def unpack(box):
    rows = box.shape[0] - PAD
    code = box[pl.ds(rows, PAD)].astype(jnp.int32).astype(jnp.float32)[0:1]
    scale = jnp.exp2(code * (1.0 / STEPS))
    return box[pl.ds(0, rows)].astype(jnp.int32).astype(jnp.float32) * (1.0 / LEVELS) * scale


def kernel(
    n_blk, line, group,
    x_ref, vals_hbm, cols, table, w_ref, out_ref,
    vals, chain, own, sib_send, sib_recv, box_send, up_recv, down_recv,
    vals_sem, x_send_sem, x_recv_sem, sib_send_sem, sib_recv_sem,
    box_send_sem, up_sem, down_sem, *pieces,
):
    slots = vals.shape[1]
    width = x_ref.shape[2]
    blk = lax.axis_index("blk")
    rep = lax.axis_index("rep")
    place = rep // 2
    core = rep % 2
    sibling = {"rep": place * 2 + 1 - core}
    above = {"rep": rep + 2}
    below = {"rep": rep - 2}

    for turn in range(n_blk):
        j = flip(blk, back(turn, n_blk), n_blk)
        load = pltpu.make_async_copy(vals_hbm.at[j], vals.at[j], vals_sem.at[turn])
        load.start()

    barrier = pltpu.get_barrier_semaphore()
    for turn in range(1, n_blk):
        pl.semaphore_signal(
            barrier, inc=1, device_id={"blk": flip(blk, turn, n_blk)}, device_id_type=MESH
        )
    pl.semaphore_signal(barrier, inc=1, device_id=sibling, device_id_type=MESH)

    @pl.when(place < line - 1)
    def _():
        pl.semaphore_signal(barrier, inc=1, device_id=above, device_id_type=MESH)

    @pl.when(place > 0)
    def _():
        pl.semaphore_signal(barrier, inc=1, device_id=below, device_id_type=MESH)

    peers = n_blk + jnp.where(place > 0, 1, 0) + jnp.where(place < line - 1, 1, 0)
    pl.semaphore_wait(barrier, peers)

    sends = []
    for turn in range(1, n_blk):
        send = pltpu.make_async_remote_copy(
            src_ref=x_ref,
            dst_ref=pieces[turn - 1],
            send_sem=x_send_sem.at[turn],
            recv_sem=x_recv_sem.at[turn],
            device_id={"blk": flip(blk, turn, n_blk)},
            device_id_type=MESH,
        )
        send.start()
        sends.append(send)

    chain[n_blk * slots] = jnp.zeros((BS, width), jnp.float32)

    batch = max(u for u in (1, 2, 4, 5, 8) if slots % u == 0)
    for turn in range(n_blk):
        j = flip(blk, back(turn, n_blk), n_blk)
        if turn:
            pltpu.make_async_remote_copy(
                src_ref=x_ref,
                dst_ref=pieces[turn - 1],
                send_sem=x_send_sem.at[turn],
                recv_sem=x_recv_sem.at[turn],
                device_id=sibling,
                device_id_type=MESH,
            ).wait_recv()
        pltpu.make_async_copy(vals_hbm.at[j], vals.at[j], vals_sem.at[turn]).wait()

        piece = pieces[turn - 1] if turn else x_ref

        def some(g, carry, j=j, piece=piece):
            first = g * batch
            products = [
                jnp.dot(
                    vals[j, first + u],
                    piece[cols[j, first + u]],
                    preferred_element_type=jnp.float32,
                )
                for u in range(batch)
            ]
            for u in range(batch):
                chain[j * slots + first + u] = products[u] + chain[table[j, first + u]]
            return carry

        lax.fori_loop(0, slots // batch, some, 0)

    def block_sum(k):
        total = chain[table[0, slots + k]]
        for j in range(1, n_blk):
            total = total + chain[table[j, slots + k]]
        return total

    def sib_copy(d):
        return pltpu.make_async_remote_copy(
            src_ref=sib_send.at[d],
            dst_ref=sib_recv.at[d],
            send_sem=sib_send_sem.at[d],
            recv_sem=sib_recv_sem.at[d],
            device_id=sibling,
            device_id_type=MESH,
        )

    lower = place < line // 2

    def gather(i, carry):
        d = jnp.where(lower, line - 1 - i, i)
        for g in range(group):
            sib_send[d, g * BS:(g + 1) * BS] = block_sum((2 * d + 1 - core) * group + g)
        sib_copy(d).start()
        for g in range(group):
            own[d, g * BS:(g + 1) * BS] = block_sum((2 * d + core) * group + g)
        return carry

    lax.fori_loop(0, line, gather, 0)

    def up_copy(d):
        return pltpu.make_async_remote_copy(
            src_ref=box_send.at[d],
            dst_ref=up_recv.at[d],
            send_sem=box_send_sem.at[d],
            recv_sem=up_sem.at[d],
            device_id=above,
            device_id_type=MESH,
        )

    def down_copy(d):
        return pltpu.make_async_remote_copy(
            src_ref=box_send.at[d],
            dst_ref=down_recv.at[d],
            send_sem=box_send_sem.at[d],
            recv_sem=down_sem.at[d],
            device_id=below,
            device_id_type=MESH,
        )

    def step(s, carry):
        @pl.when(place <= s)
        def _():
            d = line - 1 - s + place
            sib_copy(d).wait_recv()
            own[d] = own[d] + sib_recv[d]

            @pl.when(place > 0)
            def _():
                up_copy(d).wait_recv()
                own[d] = own[d] + unpack(up_recv.at[d])

            pack(own[d], box_send.at[d])
            up_copy(d).start()

        @pl.when(line - 1 - place <= s)
        def _():
            d = s - (line - 1) + place
            sib_copy(d).wait_recv()
            own[d] = own[d] + sib_recv[d]

            @pl.when(place < line - 1)
            def _():
                down_copy(d).wait_recv()
                own[d] = own[d] + unpack(down_recv.at[d])

            pack(own[d], box_send.at[d])
            down_copy(d).start()

        return carry

    lax.fori_loop(0, line - 1, step, 0)

    sib_copy(place).wait_recv()
    own[place] = own[place] + sib_recv[place]

    @pl.when(place > 0)
    def _():
        up_copy(place).wait_recv()
        own[place] = own[place] + unpack(up_recv.at[place])

    @pl.when(place < line - 1)
    def _():
        down_copy(place).wait_recv()
        own[place] = own[place] + unpack(down_recv.at[place])

    total = own[place]
    high = total.astype(jnp.bfloat16)
    low = (total - high.astype(jnp.float32)).astype(jnp.bfloat16)
    w = w_ref[...]
    result = jnp.dot(high, w, preferred_element_type=jnp.float32) + jnp.dot(
        low, w, preferred_element_type=jnp.float32
    )
    out_ref[...] = jnp.maximum(result, 0.0).astype(jnp.bfloat16)

    for send in sends:
        send.wait_send()

    def finish(d, carry):
        sib_copy(d).wait_send()

        @pl.when(d > place)
        def _():
            up_copy(d).wait_send()

        @pl.when(d < place)
        def _():
            down_copy(d).wait_send()

        return carry

    lax.fori_loop(0, line, finish, 0)


def local(node_feats, block_vals, block_rows, block_cols, block_count, weight):
    n_blk = lax.axis_size("blk")
    line = lax.axis_size("rep") // 2
    width = node_feats.shape[1]
    x = node_feats.reshape(-1, BS, width)
    group = x.shape[0]
    vals = block_vals[0, 0]
    rows = block_rows[0, 0]
    cols = block_cols[0, 0]
    count = block_count[0, 0]
    slots = rows.shape[1]
    panel = group * 2 * line

    wanted = jnp.concatenate(
        [rows, jnp.broadcast_to(jnp.arange(panel, dtype=jnp.int32), (n_blk, panel))], axis=1
    )
    spot = jnp.arange(slots, dtype=jnp.int32)
    bound = jnp.minimum(jnp.arange(slots + panel, dtype=jnp.int32), slots)
    hit = (
        (rows[:, None, :] == wanted[:, :, None])
        & (spot[None, None, :] < bound[None, :, None])
        & (spot[None, None, :] < count[:, None, None])
    )
    best = jnp.max(jnp.where(hit, spot[None, None, :], -1), axis=2)
    base = jnp.arange(n_blk, dtype=jnp.int32)[:, None] * slots
    table = jnp.where(best < 0, n_blk * slots, base + best)

    unit = group * BS
    vmem = pl.BlockSpec(memory_space=pltpu.VMEM)
    smem = pl.BlockSpec(memory_space=pltpu.SMEM)
    dma = pltpu.SemaphoreType.DMA
    return pl.pallas_call(
        functools.partial(kernel, n_blk, line, group),
        out_shape=jax.ShapeDtypeStruct((unit, weight.shape[1]), jnp.bfloat16),
        in_specs=[vmem, pl.BlockSpec(memory_space=pl.ANY), smem, smem, vmem],
        out_specs=vmem,
        scratch_shapes=[
            pltpu.VMEM(vals.shape, jnp.bfloat16),
            pltpu.VMEM((n_blk * slots + 1, BS, width), jnp.float32),
            pltpu.VMEM((line, unit, width), jnp.float32),
            pltpu.VMEM((line, unit, width), jnp.float32),
            pltpu.VMEM((line, unit, width), jnp.float32),
            pltpu.VMEM((line, unit + PAD, width), jnp.int16),
            pltpu.VMEM((line, unit + PAD, width), jnp.int16),
            pltpu.VMEM((line, unit + PAD, width), jnp.int16),
            dma((n_blk,)), dma((n_blk,)), dma((n_blk,)),
            dma((line,)), dma((line,)), dma((line,)), dma((line,)), dma((line,)),
        ]
        + [pltpu.VMEM((group, BS, width), jnp.bfloat16)] * (n_blk - 1),
        compiler_params=pltpu.CompilerParams(
            collective_id=0, has_side_effects=True, vmem_limit_bytes=56 * 1024 * 1024
        ),
        cost_estimate=pl.CostEstimate(
            flops=2 * n_blk * slots * BS * BS * width,
            bytes_accessed=2 * n_blk * slots * BS * BS,
            transcendentals=0,
        ),
    )(x, vals, cols, table, weight)


def solution(mesh):
    return jax.shard_map(
        local,
        mesh=mesh,
        in_specs=(
            P(("blk", "rep"), None),
            P("blk", "rep", None, None, None, None),
            P("blk", "rep", None, None),
            P("blk", "rep", None, None),
            P("blk", "rep", None),
            P(),
        ),
        out_specs=P(("blk", "rep"), None),
        check_vma=False,
    )
```

time: 83 us -> 34.2 us (0.41)
  waiting for transfers between devices: 38.6 us -> 0 us
  Pallas kernels: 0 us -> 29.4 us
  matrix products: 19.1 us -> 0 us
  between operations: 13.5 us -> 0.02 us
  starting transfers between devices: 5.32 us -> 0 us
  local copies, waits for them, and re-layouts: 3.75 us -> 1.62 us
    reduce_scatter x1 -> x0, waiting for transfers between devices: 34.8 us -> none  [local(): lax.psum_scatter(flat_panel, 'rep', scatter_dimension=0, tiled=True)]
    pallas_call x0 -> x1, Pallas kernels: none -> 29.4 us  [local(): pl.pallas_call(functools.partial(kernel, n_blk, line, group), out_shape=j...]
    dot_general x13 -> x0, matrix products: 19.1 us -> none  [the longest x4 10.6 us: add_blocks(): jnp.einsum('sk,saf->kaf', row_select, products, precision=lax.Precision.H...]
    ppermute x3 -> x0, starting transfers between devices: 5.31 us -> none  [shifted(): lax.ppermute(array, axis, [(i, (i + by) % size) for i in range(size)])]
    ppermute x3 -> x0, waiting for transfers between devices: 3.8 us -> none  [shifted(): lax.ppermute(array, axis, [(i, (i + by) % size) for i in range(size)])]
    lt x4 -> x2, other arithmetic: 2.53 us -> 0.73 us  [the longest x1 0.73 us: local(): spot[None, None, :] < count[:, None, None]]
    unnamed x4 -> x1, local copies, waits for them, and re-layouts: 0.01 us -> 1.62 us
    dynamic_slice x1 -> x0, local copies, waits for them, and re-layouts: 1.46 us -> none  [absorb(): live_count = lax.dynamic_index_in_dim(list_count, source, 0, keepdims=False)]
  transfers between devices with their start and end apart: 4 -> 0, of which waited for: 3 -> 0; matrix products, arithmetic and copies ran while one was open for 16% -> 0% of each run, Pallas kernels for 0% -> 0%
where the time goes in v1:
time: 34.2 us; the launch traced here: 34 us
  Pallas kernels  29.4 us (86%)
  other arithmetic  2.96 us (9%)
  local copies, waits for them, and re-layouts  1.62 us (5%)
    pallas_call x1, Pallas kernels, local(): pl.pallas_call(functools.partial(kernel, n_blk, line, group), out_shape=j...  29.4 us
    unnamed x1, local copies, waits for them, and re-layouts  1.62 us
    reduce_max x1, other arithmetic, local(): best = jnp.max(jnp.where(hit, spot[None, None, :], -1), axis=2)  0.81 us
    concatenate x1, other arithmetic, local(): jnp.concatenate([rows, jnp.broadcast_to(jnp.arange(panel, dtype=jnp.int32...  0.76 us
    lt x1, other arithmetic, local(): spot[None, None, :] < count[:, None, None]  0.73 us

profile of v1, /device:TPU:0, one launch (start us, length us, event | category | flops | bytes accessed | tf_op | source)
XLA Modules:
  0.0 34.0 jit_solution(18112910809348045408)
XLA Ops:
  0.0 0.7 %iota_compare_fusion.1 = pred[4,40]{1,0:T(4,128)(4,1)S(1)} fusion(s32[4]{0:T(128)} %bitcast.10), kind=kLoop, calls=%fused_computation.4 | loop fusion | flops 160 | bytes 176 | tf_op jit(solution)/shard_map/lt | solution.py:284
  0.7 0.8 %pad_add_fusion = s32[4,64]{1,0:T(4,128)S(1)} fusion(s32[4,24]{1,0:T(4,128)S(1)} %broadcast_in_dim.25, s32[4,40]{1,0:T(4,128)} %bitcast.7), kind=kLoop, calls=%fused_computation.2 | loop fusion | flops 256 | bytes 2048 | tf_op jit(solution)/shard_map/concatenate | solution.py:276
  1.5 0.8 %select_reduce_fusion = s32[4,64]{1,0:T(4,128)S(1)} fusion(s32[4,64]{1,0:T(4,128)S(1)} %pad_add_fusion, s32[4,40]{1,0:T(4,128)} %bitcast.8, pred[4,40]{1,0:T(4,128)(4,1)S(1)} %iota_compare_fusion.1, pred[64,40]{0,1:T(8,128)(4,1)S(1)} %iota_compare_fusion), kind=kLoop, calls=%fused_computation | loop fusion | flops 50944 | bytes 5408 | tf_op jit(solution)/shard_map/reduce_max | solution.py:286
  2.3 0.7 %add_select_fusion.table = s32[4,64]{1,0:T(4,128)} fusion(s32[4,64]{1,0:T(4,128)S(1)} %select_reduce_fusion, s32[4]{0:T(128)S(1)} %iota_multiply_fusion), kind=kLoop, calls=%fused_computation.3 | loop fusion | flops 768 | bytes 2064 | tf_op jit(solution)/shard_map/jit(_where)/select_n | solution.py:288
  3.0 29.4 %shard_map.64 = bf16[384,256]{1,0:T(8,128)(2,1)} custom-call(bf16[3,128,128]{2,1,0:T(8,128)(2,1)} %bitcast.6, bf16[4,40,128,128]{3,2,1,0:T(8,128)(2,1)} %bitcast.5, s32[4,40]{1,0:T(4,128)} %bitcast.9, s32[4,64]{1,0:T(4,128)} %add_select_fusion.table, bf16[128,256]{1,0:T(8,128)(2,1)} %w_ref.1), custom_call_target="tpu_custom_call" | custom-call | flops 671088640 | bytes 5242880 | tf_op jit(solution)/shard_map/pallas_call | solution.py:294
  32.3 1.6 %copy.8 = bf16[384,256]{1,0:T(8,128)(2,1)} copy(bf16[384,256]{1,0:T(8,128)(2,1)} %shard_map.64) | data formatting | bytes 393216
  (4 shorter events, 0.0 us)

commit v2 on v1

--- a/solution.py
+++ b/solution.py
@@ -50,14 +50,46 @@
     return box[pl.ds(0, rows)].astype(jnp.int32).astype(jnp.float32) * (1.0 / LEVELS) * scale
 
 
+def prepare(rows_ref, cols_ref, count, prep, panel):
+    lists, slots = rows_ref.shape
+    lane = lax.broadcasted_iota(jnp.int32, (slots, slots), 1)
+    sub = lax.broadcasted_iota(jnp.int32, (slots, slots), 0)
+    place = lax.broadcasted_iota(jnp.int32, (slots, panel), 1)
+
+    def upright(line):
+        spread = jnp.broadcast_to(line, (slots, slots))
+        return jnp.sum(jnp.where(lane == sub, spread, 0), axis=1, keepdims=True)
+
+    prep[...] = jnp.zeros(prep.shape, jnp.int32)
+    for j in range(lists):
+        key = jnp.where(lane[0:1] < count[j], rows_ref[j:j + 1, :], panel)
+        unique = key * slots + lane[0:1]
+        key_up = upright(key)
+        col_up = upright(cols_ref[j:j + 1, :])
+        unique_up = key_up * slots + sub[:, 0:1]
+        rank = jnp.sum(jnp.where(unique < unique_up, 1, 0), axis=1, keepdims=True)
+        again = jnp.logical_and(key == key_up, lane < sub)
+        keep_up = jnp.max(jnp.where(again, 1, 0), axis=1, keepdims=True)
+        here = rank == lane
+        for at, entry in enumerate((sub, col_up, keep_up)):
+            prep[j, at:at + 1, 0:slots] = jnp.sum(
+                jnp.where(here, entry, 0), axis=0, keepdims=True
+            )
+        upto = jnp.sum(jnp.where(key_up <= place, 1, 0), axis=0, keepdims=True)
+        found = jnp.max(jnp.where(key_up == place, 1, 0), axis=0, keepdims=True)
+        prep[j, 3:4, 0:panel] = jnp.where(found > 0, upto + (j * slots - 1), lists * slots)
+
+
 def kernel(
     n_blk, line, group,
-    x_ref, vals_hbm, cols, table, w_ref, out_ref,
-    vals, chain, own, sib_send, sib_recv, box_send, up_recv, down_recv,
+    x_ref, vals_hbm, rows_ref, cols_ref, count, w_ref, out_ref,
+    prep, table, chain, own, sib_send, sib_recv, box_send, up_recv, down_recv,
     vals_sem, x_send_sem, x_recv_sem, sib_send_sem, sib_recv_sem,
-    box_send_sem, up_sem, down_sem, *pieces,
+    box_send_sem, up_sem, down_sem, table_sem, *pieces_and_vals,
 ):
-    slots = vals.shape[1]
+    pieces = (x_ref,) + pieces_and_vals[:n_blk - 1]
+    vals = pieces_and_vals[n_blk - 1:]
+    slots = vals_hbm.shape[1]
     width = x_ref.shape[2]
     blk = lax.axis_index("blk")
     rep = lax.axis_index("rep")
@@ -69,7 +101,7 @@
 
     for turn in range(n_blk):
         j = flip(blk, back(turn, n_blk), n_blk)
-        load = pltpu.make_async_copy(vals_hbm.at[j], vals.at[j], vals_sem.at[turn])
+        load = pltpu.make_async_copy(vals_hbm.at[j], vals[turn], vals_sem.at[turn])
         load.start()
 
     barrier = pltpu.get_barrier_semaphore()
@@ -87,6 +119,10 @@
     def _():
         pl.semaphore_signal(barrier, inc=1, device_id=below, device_id_type=MESH)
 
+    prepare(rows_ref, cols_ref, count, prep, group * 2 * line)
+    fill = pltpu.make_async_copy(prep, table, table_sem)
+    fill.start()
+
     peers = n_blk + jnp.where(place > 0, 1, 0) + jnp.where(place < line - 1, 1, 0)
     pl.semaphore_wait(barrier, peers)
 
@@ -94,7 +130,7 @@
     for turn in range(1, n_blk):
         send = pltpu.make_async_remote_copy(
             src_ref=x_ref,
-            dst_ref=pieces[turn - 1],
+            dst_ref=pieces[turn],
             send_sem=x_send_sem.at[turn],
             recv_sem=x_recv_sem.at[turn],
             device_id={"blk": flip(blk, turn, n_blk)},
@@ -105,42 +141,39 @@
 
     chain[n_blk * slots] = jnp.zeros((BS, width), jnp.float32)
 
-    batch = max(u for u in (1, 2, 4, 5, 8) if slots % u == 0)
+    fill.wait()
+    batch = max(u for u in range(1, 21) if slots % u == 0)
     for turn in range(n_blk):
         j = flip(blk, back(turn, n_blk), n_blk)
+        pltpu.make_async_copy(vals_hbm.at[j], vals[turn], vals_sem.at[turn]).wait()
         if turn:
             pltpu.make_async_remote_copy(
                 src_ref=x_ref,
-                dst_ref=pieces[turn - 1],
+                dst_ref=pieces[turn],
                 send_sem=x_send_sem.at[turn],
                 recv_sem=x_recv_sem.at[turn],
                 device_id=sibling,
                 device_id_type=MESH,
             ).wait_recv()
-        pltpu.make_async_copy(vals_hbm.at[j], vals.at[j], vals_sem.at[turn]).wait()
-
-        piece = pieces[turn - 1] if turn else x_ref
-
-        def some(g, carry, j=j, piece=piece):
-            first = g * batch
-            products = [
-                jnp.dot(
-                    vals[j, first + u],
-                    piece[cols[j, first + u]],
+
+        def some(g, total, j=j, piece=pieces[turn], blocks=vals[turn]):
+            for u in range(batch):
+                t = g * batch + u
+                product = jnp.dot(
+                    blocks[table[j, 0, t]],
+                    piece[table[j, 1, t]],
                     preferred_element_type=jnp.float32,
                 )
-                for u in range(batch)
-            ]
-            for u in range(batch):
-                chain[j * slots + first + u] = products[u] + chain[table[j, first + u]]
-            return carry
-
-        lax.fori_loop(0, slots // batch, some, 0)
+                total = total * table[j, 2, t].astype(jnp.float32) + product
+                chain[j * slots + t] = total
+            return total
+
+        lax.fori_loop(0, slots // batch, some, jnp.zeros((BS, width), jnp.float32))
 
     def block_sum(k):
-        total = chain[table[0, slots + k]]
+        total = chain[table[0, 3, k]]
         for j in range(1, n_blk):
-            total = total + chain[table[j, slots + k]]
+            total = total + chain[table[j, 3, k]]
         return total
 
     def sib_copy(d):
@@ -271,22 +304,6 @@
     cols = block_cols[0, 0]
     count = block_count[0, 0]
     slots = rows.shape[1]
-    panel = group * 2 * line
-
-    wanted = jnp.concatenate(
-        [rows, jnp.broadcast_to(jnp.arange(panel, dtype=jnp.int32), (n_blk, panel))], axis=1
-    )
-    spot = jnp.arange(slots, dtype=jnp.int32)
-    bound = jnp.minimum(jnp.arange(slots + panel, dtype=jnp.int32), slots)
-    hit = (
-        (rows[:, None, :] == wanted[:, :, None])
-        & (spot[None, None, :] < bound[None, :, None])
-        & (spot[None, None, :] < count[:, None, None])
-    )
-    best = jnp.max(jnp.where(hit, spot[None, None, :], -1), axis=2)
-    base = jnp.arange(n_blk, dtype=jnp.int32)[:, None] * slots
-    table = jnp.where(best < 0, n_blk * slots, base + best)
-
     unit = group * BS
     vmem = pl.BlockSpec(memory_space=pltpu.VMEM)
     smem = pl.BlockSpec(memory_space=pltpu.SMEM)
@@ -294,10 +311,11 @@
     return pl.pallas_call(
         functools.partial(kernel, n_blk, line, group),
         out_shape=jax.ShapeDtypeStruct((unit, weight.shape[1]), jnp.bfloat16),
-        in_specs=[vmem, pl.BlockSpec(memory_space=pl.ANY), smem, smem, vmem],
+        in_specs=[vmem, pl.BlockSpec(memory_space=pl.ANY), vmem, vmem, smem, vmem],
         out_specs=vmem,
         scratch_shapes=[
-            pltpu.VMEM(vals.shape, jnp.bfloat16),
+            pltpu.VMEM((n_blk, 8, 128), jnp.int32),
+            pltpu.SMEM((n_blk, 8, 128), jnp.int32),
             pltpu.VMEM((n_blk * slots + 1, BS, width), jnp.float32),
             pltpu.VMEM((line, unit, width), jnp.float32),
             pltpu.VMEM((line, unit, width), jnp.float32),
@@ -307,8 +325,10 @@
             pltpu.VMEM((line, unit + PAD, width), jnp.int16),
             dma((n_blk,)), dma((n_blk,)), dma((n_blk,)),
             dma((line,)), dma((line,)), dma((line,)), dma((line,)), dma((line,)),
+            dma,
         ]
-        + [pltpu.VMEM((group, BS, width), jnp.bfloat16)] * (n_blk - 1),
+        + [pltpu.VMEM((group, BS, width), jnp.bfloat16)] * (n_blk - 1)
+        + [pltpu.VMEM(vals.shape[1:], jnp.bfloat16)] * n_blk,
         compiler_params=pltpu.CompilerParams(
             collective_id=0, has_side_effects=True, vmem_limit_bytes=56 * 1024 * 1024
         ),
@@ -317,7 +337,7 @@
             bytes_accessed=2 * n_blk * slots * BS * BS,
             transcendentals=0,
         ),
-    )(x, vals, cols, table, weight)
+    )(x, vals, rows, cols, count, weight)
 
 
 def solution(mesh):

time: 34.2 us -> 29.9 us (0.87)
  other arithmetic: 2.96 us -> 0 us
  Pallas kernels: 29.4 us -> 28.2 us
    pallas_call x1, Pallas kernels: 29.4 us -> 28.2 us  [local(): pl.pallas_call(functools.partial(kernel, n_blk, line, group), out_shape=j...]
    reduce_max x1 -> x0, other arithmetic: 0.81 us -> none  [local(): best = jnp.max(jnp.where(hit, spot[None, None, :], -1), axis=2)]
    concatenate x1 -> x0, other arithmetic: 0.76 us -> none  [local(): jnp.concatenate([rows, jnp.broadcast_to(jnp.arange(panel, dtype=jnp.int32...]
    lt x2 -> x0, other arithmetic: 0.73 us -> none  [the longest x1 0.73 us: local(): spot[None, None, :] < count[:, None, None]]
    select_n x1 -> x0, other arithmetic: 0.65 us -> none  [local(): table = jnp.where(best < 0, n_blk * slots, base + best)]
where the time goes in v2:
time: 29.9 us; the launch traced here: 29.8 us
  Pallas kernels  28.2 us (94%)
  local copies, waits for them, and re-layouts  1.62 us (5%)
    pallas_call x1, Pallas kernels, local(): pl.pallas_call(functools.partial(kernel, n_blk, line, group), out_shape=j...  28.2 us
    unnamed x1, local copies, waits for them, and re-layouts  1.62 us

profile of v2, /device:TPU:0, one launch (start us, length us, event | category | flops | bytes accessed | tf_op | source)
XLA Modules:
  0.0 29.8 jit_solution(10575160189140284783)
XLA Ops:
  0.0 28.2 %shard_map.64 = bf16[384,256]{1,0:T(8,128)(2,1)} custom-call(bf16[3,128,128]{2,1,0:T(8,128)(2,1)} %bitcast.6, bf16[4,40,128,128]{3,2,1,0:T(8,128)(2,1)} %bitcast.5, s32[4,40]{1,0:T(4,128)} %bitcast.7, s32[4,40]{1,0:T(4,128)} %bitcast.8, s32[4]{0:T(128)} %bitcast.9, bf16[128,256]{1,0:T(8,128)(2,1)} %w_ref.1), custom_call_target="tpu_custom_call" | custom-call | flops 671088640 | bytes 5242880 | tf_op jit(solution)/shard_map/pallas_call | solution.py:311
  28.2 1.6 %copy.8 = bf16[384,256]{1,0:T(8,128)(2,1)} copy(bf16[384,256]{1,0:T(8,128)(2,1)} %shard_map.64) | data formatting | bytes 393216

commit v3 on v2

v3 whole, which is shorter than its diff:
```python
import functools

import jax
import jax.numpy as jnp
from jax import lax
from jax.experimental import pallas as pl
from jax.experimental.pallas import tpu as pltpu
from jax.sharding import PartitionSpec as P

BS = 128
LEVELS = 32000.0
STEPS = 256.0
TINY = 1e-36
PAD = 16
MESH = pl.DeviceIdType.MESH


def flip(index, mask, size):
    if size & (size - 1):
        return (index + mask) % size
    out = index
    bit = 1
    while bit < size:
        if mask & bit:
            out = out + bit * (1 - 2 * ((index // bit) % 2))
        bit *= 2
    return out


def back(mask, size):
    return (size - mask) % size if size & (size - 1) else mask


def scale_of(code):
    return jnp.exp2(code * (1.0 / STEPS))


def read_code(box):
    return box[pl.ds(0, PAD)].astype(jnp.int32).astype(jnp.float32)[0:1]


def decode(box, g, scale):
    part = box[pl.ds(PAD + g * BS, BS)].astype(jnp.int32).astype(jnp.float32)
    return part * (1.0 / LEVELS) * scale


def prepare(rows_ref, cols_ref, count_ref, prep, panel, group):
    lists, slots = rows_ref.shape
    lane = lax.broadcasted_iota(jnp.int32, (slots, slots), 1)
    sub = lax.broadcasted_iota(jnp.int32, (slots, slots), 0)
    place = lax.broadcasted_iota(jnp.int32, (slots, panel), 1)
    col_bits = max(1, (group - 1).bit_length())
    slot_bits = max(1, (slots - 1).bit_length())
    row_bits = col_bits + slot_bits

    for j in range(lists):
        live = lane[0:1] < count_ref[0:1, j:j + 1]
        key = jnp.where(live, rows_ref[j:j + 1, :], panel)
        col = jnp.where(live, cols_ref[j:j + 1, :], 0)
        word = key * (1 << row_bits) + lane[0:1] * (1 << col_bits) + col
        spread = jnp.broadcast_to(word, (slots, slots))
        word_up = jnp.sum(jnp.where(lane == sub, spread, 0), axis=1, keepdims=True)
        rank = jnp.sum(jnp.where(word < word_up, 1, 0), axis=1, keepdims=True)
        key_up = word_up >> row_bits
        before = jnp.max(jnp.where(rank == lane - 1, key_up, -1), axis=0, keepdims=True)
        ordered = jnp.sum(jnp.where(rank == lane, word_up, 0), axis=0, keepdims=True)
        prep[j, 0:1, 0:slots] = (ordered >> col_bits) & ((1 << slot_bits) - 1)
        prep[j, 1:2, 0:slots] = ordered & ((1 << col_bits) - 1)
        prep[j, 2:3, 0:slots] = jnp.where(before == (ordered >> row_bits), 1, 0)
        upto = jnp.sum(jnp.where(key_up <= place, 1, 0), axis=0, keepdims=True)
        found = jnp.max(jnp.where(key_up == place, 1, 0), axis=0, keepdims=True)
        prep[j, 3:4, 0:panel] = jnp.where(found > 0, upto + (j * slots - 1), lists * slots)


def kernel(
    n_blk, line, group,
    x_hbm, vals_hbm, rows_hbm, cols_hbm, count_hbm, w_hbm, out_ref,
    rows_ref, cols_ref, count_ref, w_ref, prep, table, chain, own, sib_send, sib_recv, box_send, up_recv, down_recv,
    vals_sem, x_send_sem, x_recv_sem, sib_send_sem, sib_recv_sem,
    box_send_sem, up_sem, down_sem, table_sem, in_sem, *pieces_and_vals,
):
    pieces = pieces_and_vals[:n_blk]
    vals = pieces_and_vals[n_blk:]
    slots = vals_hbm.shape[1]
    width = x_hbm.shape[2]
    blk = lax.axis_index("blk")
    rep = lax.axis_index("rep")
    place = rep // 2
    core = rep % 2
    sibling = {"rep": place * 2 + 1 - core}
    above = {"rep": rep + 2}
    below = {"rep": rep - 2}

    barrier = pltpu.get_barrier_semaphore()
    for turn in range(1, n_blk):
        pl.semaphore_signal(
            barrier, inc=1, device_id={"blk": flip(blk, turn, n_blk)}, device_id_type=MESH
        )
    pl.semaphore_signal(barrier, inc=1, device_id=sibling, device_id_type=MESH)

    @pl.when(place < line - 1)
    def _():
        pl.semaphore_signal(barrier, inc=1, device_id=above, device_id_type=MESH)

    @pl.when(place > 0)
    def _():
        pl.semaphore_signal(barrier, inc=1, device_id=below, device_id_type=MESH)

    fetches = [
        pltpu.make_async_copy(source, target, in_sem.at[i])
        for i, (source, target) in enumerate((
            (rows_hbm, rows_ref),
            (cols_hbm, cols_ref),
            (count_hbm, count_ref),
            (x_hbm, pieces[0]),
            (w_hbm, w_ref),
        ))
    ]
    for fetch in fetches:
        fetch.start()

    for turn in range(n_blk):
        j = flip(blk, back(turn, n_blk), n_blk)
        load = pltpu.make_async_copy(vals_hbm.at[j], vals[turn], vals_sem.at[turn])
        load.start()

    peers = n_blk + jnp.where(place > 0, 1, 0) + jnp.where(place < line - 1, 1, 0)
    pl.semaphore_wait(barrier, peers)

    sends = []
    for turn in range(1, n_blk):
        send = pltpu.make_async_remote_copy(
            src_ref=x_hbm,
            dst_ref=pieces[turn],
            send_sem=x_send_sem.at[turn],
            recv_sem=x_recv_sem.at[turn],
            device_id={"blk": flip(blk, turn, n_blk)},
            device_id_type=MESH,
        )
        send.start()
        sends.append(send)

    prep[...] = jnp.zeros(prep.shape, jnp.int32)
    for fetch in fetches[:3]:
        fetch.wait()
    prepare(rows_ref, cols_ref, count_ref, prep, group * 2 * line, group)
    fill = pltpu.make_async_copy(prep, table, table_sem)
    fill.start()
    chain[n_blk * slots] = jnp.zeros((BS, width), jnp.float32)

    fill.wait()
    for fetch in fetches[3:]:
        fetch.wait()
    batch = max(u for u in range(1, 21) if slots % u == 0)
    for turn in range(n_blk):
        j = flip(blk, back(turn, n_blk), n_blk)
        pltpu.make_async_copy(vals_hbm.at[j], vals[turn], vals_sem.at[turn]).wait()
        if turn:
            pltpu.make_async_remote_copy(
                src_ref=x_hbm,
                dst_ref=pieces[turn],
                send_sem=x_send_sem.at[turn],
                recv_sem=x_recv_sem.at[turn],
                device_id=sibling,
                device_id_type=MESH,
            ).wait_recv()

        def some(g, total, j=j, piece=pieces[turn], blocks=vals[turn]):
            for u in range(batch):
                t = g * batch + u
                product = jnp.dot(
                    blocks[table[j, 0, t]],
                    piece[table[j, 1, t]],
                    preferred_element_type=jnp.float32,
                )
                total = total * table[j, 2, t].astype(jnp.float32) + product
                chain[j * slots + t] = total
            return total

        lax.fori_loop(0, slots // batch, some, jnp.zeros((BS, width), jnp.float32))

    def block_sum(k):
        total = chain[table[0, 3, k]]
        for j in range(1, n_blk):
            total = total + chain[table[j, 3, k]]
        return total

    def sib_copy(d):
        return pltpu.make_async_remote_copy(
            src_ref=sib_send.at[d],
            dst_ref=sib_recv.at[d],
            send_sem=sib_send_sem.at[d],
            recv_sem=sib_recv_sem.at[d],
            device_id=sibling,
            device_id_type=MESH,
        )

    lower = place < line // 2

    def gather(i, carry):
        d = jnp.where(lower, line - 1 - i, i)
        for g in range(group):
            sib_send[d, g * BS:(g + 1) * BS] = block_sum((2 * d + 1 - core) * group + g)
        sib_copy(d).start()
        for g in range(group):
            own[d, g * BS:(g + 1) * BS] = block_sum((2 * d + core) * group + g)
        return carry

    lax.fori_loop(0, line, gather, 0)

    def rows_of(g):
        return pl.ds(0, PAD + BS) if g == 0 else pl.ds(PAD + g * BS, BS)

    def up_copy(d, g):
        return pltpu.make_async_remote_copy(
            src_ref=box_send.at[d, rows_of(g)],
            dst_ref=up_recv.at[d, rows_of(g)],
            send_sem=box_send_sem.at[d, g],
            recv_sem=up_sem.at[d, g],
            device_id=above,
            device_id_type=MESH,
        )

    def down_copy(d, g):
        return pltpu.make_async_remote_copy(
            src_ref=box_send.at[d, rows_of(g)],
            dst_ref=down_recv.at[d, rows_of(g)],
            send_sem=box_send_sem.at[d, g],
            recv_sem=down_sem.at[d, g],
            device_id=below,
            device_id_type=MESH,
        )

    def hop(d, copy, box, first):
        sib_copy(d).wait_recv()
        both = own[d] + sib_recv[d]
        own[d] = both
        top = jnp.max(jnp.abs(both), axis=0, keepdims=True)
        if not first:
            copy(d, 0).wait_recv()
            scale = scale_of(read_code(box.at[d]))
            top = top + scale
        code = jnp.ceil(jnp.log2(jnp.maximum(top, TINY)) * STEPS)
        inverse = 1.0 / scale_of(code)
        box_send[d, 0:PAD] = (
            jnp.broadcast_to(code, (PAD, width)).astype(jnp.int32).astype(jnp.int16)
        )
        for g in range(group):
            total = own[d, g * BS:(g + 1) * BS]
            if not first:
                if g:
                    copy(d, g).wait_recv()
                total = total + decode(box.at[d], g, scale)
            whole = jnp.round(total * inverse * LEVELS).astype(jnp.int32)
            box_send[d, PAD + g * BS:PAD + (g + 1) * BS] = whole.astype(jnp.int16)
            copy(d, g).start()

    def step(s, carry):
        up_to = line - 1 - s + place
        down_to = s - (line - 1) + place

        @pl.when(jnp.logical_and(place <= s, place == 0))
        def _():
            hop(up_to, up_copy, up_recv, True)

        @pl.when(jnp.logical_and(place <= s, place > 0))
        def _():
            hop(up_to, up_copy, up_recv, False)

        @pl.when(jnp.logical_and(line - 1 - place <= s, place == line - 1))
        def _():
            hop(down_to, down_copy, down_recv, True)

        @pl.when(jnp.logical_and(line - 1 - place <= s, place < line - 1))
        def _():
            hop(down_to, down_copy, down_recv, False)

        return carry

    lax.fori_loop(0, line - 1, step, 0)

    sib_copy(place).wait_recv()
    own[place] = own[place] + sib_recv[place]
    w = w_ref[...]
    for g in range(group):
        block = pl.ds(g * BS, BS)

        @pl.when(place > 0)
        def _():
            up_copy(place, g).wait_recv()
            scale = scale_of(read_code(up_recv.at[place]))
            own[place, block] = own[place, block] + decode(up_recv.at[place], g, scale)

        @pl.when(place < line - 1)
        def _():
            down_copy(place, g).wait_recv()
            scale = scale_of(read_code(down_recv.at[place]))
            own[place, block] = own[place, block] + decode(down_recv.at[place], g, scale)

        total = own[place, block]
        high = total.astype(jnp.bfloat16)
        low = (total - high.astype(jnp.float32)).astype(jnp.bfloat16)
        result = jnp.dot(high, w, preferred_element_type=jnp.float32) + jnp.dot(
            low, w, preferred_element_type=jnp.float32
        )
        out_ref[block] = jnp.maximum(result, 0.0).astype(jnp.bfloat16)

    for send in sends:
        send.wait_send()

    def finish(d, carry):
        sib_copy(d).wait_send()

        @pl.when(d > place)
        def _():
            for g in range(group):
                up_copy(d, g).wait_send()

        @pl.when(d < place)
        def _():
            for g in range(group):
                down_copy(d, g).wait_send()

        return carry

    lax.fori_loop(0, line, finish, 0)


def local(node_feats, block_vals, block_rows, block_cols, block_count, weight):
    n_blk = lax.axis_size("blk")
    line = lax.axis_size("rep") // 2
    width = node_feats.shape[1]
    x = node_feats.reshape(-1, BS, width)
    group = x.shape[0]
    vals = block_vals[0, 0]
    rows = block_rows[0, 0]
    cols = block_cols[0, 0]
    count = block_count[0]
    slots = rows.shape[1]
    unit = group * BS
    vmem = pl.BlockSpec(memory_space=pltpu.VMEM)
    anywhere = pl.BlockSpec(memory_space=pl.ANY)
    dma = pltpu.SemaphoreType.DMA
    return pl.pallas_call(
        functools.partial(kernel, n_blk, line, group),
        out_shape=jax.ShapeDtypeStruct((unit, weight.shape[1]), jnp.bfloat16),
        in_specs=[anywhere] * 6,
        out_specs=vmem,
        scratch_shapes=[
            pltpu.VMEM(rows.shape, jnp.int32),
            pltpu.VMEM(cols.shape, jnp.int32),
            pltpu.VMEM(count.shape, jnp.int32),
            pltpu.VMEM(weight.shape, jnp.bfloat16),
            pltpu.VMEM((n_blk, 8, 128), jnp.int32),
            pltpu.SMEM((n_blk, 8, 128), jnp.int32),
            pltpu.VMEM((n_blk * slots + 1, BS, width), jnp.float32),
            pltpu.VMEM((line, unit, width), jnp.float32),
            pltpu.VMEM((line, unit, width), jnp.float32),
            pltpu.VMEM((line, unit, width), jnp.float32),
            pltpu.VMEM((line, unit + PAD, width), jnp.int16),
            pltpu.VMEM((line, unit + PAD, width), jnp.int16),
            pltpu.VMEM((line, unit + PAD, width), jnp.int16),
            dma((n_blk,)), dma((n_blk,)), dma((n_blk,)),
            dma((line,)), dma((line,)),
            dma((line, group)), dma((line, group)), dma((line, group)),
            dma, dma((5,)),
        ]
        + [pltpu.VMEM((group, BS, width), jnp.bfloat16)] * n_blk
        + [pltpu.VMEM(vals.shape[1:], jnp.bfloat16)] * n_blk,
        compiler_params=pltpu.CompilerParams(
            collective_id=0, has_side_effects=True, vmem_limit_bytes=56 * 1024 * 1024
        ),
        cost_estimate=pl.CostEstimate(
            flops=2 * n_blk * slots * BS * BS * width,
            bytes_accessed=2 * n_blk * slots * BS * BS,
            transcendentals=0,
        ),
    )(x, vals, rows, cols, count, weight)


def solution(mesh):
    return jax.shard_map(
        local,
        mesh=mesh,
        in_specs=(
            P(("blk", "rep"), None),
            P("blk", "rep", None, None, None, None),
            P("blk", "rep", None, None),
            P("blk", "rep", None, None),
            P("blk", "rep", None),
            P(),
        ),
        out_specs=P(("blk", "rep"), None),
        check_vma=False,
    )
```

time: 29.9 us -> 26.6 us (0.89)
  Pallas kernels: 28.2 us -> 24.8 us
    pallas_call x1, Pallas kernels: 28.2 us -> 24.8 us  [local(): pl.pallas_call(functools.partial(kernel, n_blk, line, group), out_shape=j...]
where the time goes in v3:
time: 26.6 us; the launch traced here: 26.4 us
  Pallas kernels  24.8 us (93%)
  local copies, waits for them, and re-layouts  1.62 us (6%)
    pallas_call x1, Pallas kernels, local(): pl.pallas_call(functools.partial(kernel, n_blk, line, group), out_shape=j...  24.8 us
    unnamed x1, local copies, waits for them, and re-layouts  1.62 us

profile of v3, /device:TPU:0, one launch (start us, length us, event | category | flops | bytes accessed | tf_op | source)
XLA Modules:
  0.0 26.4 jit_solution(14360853245133463319)
XLA Ops:
  0.0 24.8 %shard_map.64 = bf16[384,256]{1,0:T(8,128)(2,1)} custom-call(bf16[3,128,128]{2,1,0:T(8,128)(2,1)} %bitcast.6, bf16[4,40,128,128]{3,2,1,0:T(8,128)(2,1)} %bitcast.5, s32[4,40]{1,0:T(4,128)} %bitcast.7, s32[4,40]{1,0:T(4,128)} %bitcast.8, s32[1,4]{1,0:T(1,128)} %bitcast.9, bf16[128,256]{1,0:T(8,128)(2,1)} %w_hbm.1), custom_call_target="tpu_custom_call" | custom-call | flops 671088640 | bytes 5242880 | tf_op jit(solution)/shard_map/pallas_call | solution.py:344
  24.8 1.6 %copy.8 = bf16[384,256]{1,0:T(8,128)(2,1)} copy(bf16[384,256]{1,0:T(8,128)(2,1)} %shard_map.64) | data formatting | bytes 393216

commit v4 on v3

--- a/solution.py
+++ b/solution.py
@@ -91,8 +91,11 @@
     above = {"rep": rep + 2}
     below = {"rep": rep - 2}
 
+    square = n_blk == 4
+    direct = (1, 2) if square else tuple(range(1, n_blk))
+
     barrier = pltpu.get_barrier_semaphore()
-    for turn in range(1, n_blk):
+    for turn in direct:
         pl.semaphore_signal(
             barrier, inc=1, device_id={"blk": flip(blk, turn, n_blk)}, device_id_type=MESH
         )
@@ -119,26 +122,35 @@
     for fetch in fetches:
         fetch.start()
 
-    for turn in range(n_blk):
+    def load(turn):
         j = flip(blk, back(turn, n_blk), n_blk)
-        load = pltpu.make_async_copy(vals_hbm.at[j], vals[turn], vals_sem.at[turn])
-        load.start()
-
-    peers = n_blk + jnp.where(place > 0, 1, 0) + jnp.where(place < line - 1, 1, 0)
+        return pltpu.make_async_copy(vals_hbm.at[j], vals[turn], vals_sem.at[turn])
+
+    load(0).start()
+
+    peers = len(direct) + 1 + jnp.where(place > 0, 1, 0) + jnp.where(place < line - 1, 1, 0)
     pl.semaphore_wait(barrier, peers)
 
-    sends = []
+    def half(ref, h):
+        return ref.at[:, pl.ds(h * (BS // 2), BS // 2)]
+
+    def pass_on(source, turn, h, to):
+        return pltpu.make_async_remote_copy(
+            src_ref=half(source, h),
+            dst_ref=half(pieces[turn], h),
+            send_sem=x_send_sem.at[turn, h],
+            recv_sem=x_recv_sem.at[turn, h],
+            device_id={"blk": flip(blk, to, n_blk)},
+            device_id_type=MESH,
+        )
+
+    sends = [
+        pass_on(x_hbm, turn, (first + turn + 1) % 2, turn) for first in (0, 1) for turn in direct
+    ]
+    for send in sends:
+        send.start()
     for turn in range(1, n_blk):
-        send = pltpu.make_async_remote_copy(
-            src_ref=x_hbm,
-            dst_ref=pieces[turn],
-            send_sem=x_send_sem.at[turn],
-            recv_sem=x_recv_sem.at[turn],
-            device_id={"blk": flip(blk, turn, n_blk)},
-            device_id_type=MESH,
-        )
-        send.start()
-        sends.append(send)
+        load(turn).start()
 
     prep[...] = jnp.zeros(prep.shape, jnp.int32)
     for fetch in fetches[:3]:
@@ -154,16 +166,16 @@
     batch = max(u for u in range(1, 21) if slots % u == 0)
     for turn in range(n_blk):
         j = flip(blk, back(turn, n_blk), n_blk)
-        pltpu.make_async_copy(vals_hbm.at[j], vals[turn], vals_sem.at[turn]).wait()
-        if turn:
-            pltpu.make_async_remote_copy(
-                src_ref=x_hbm,
-                dst_ref=pieces[turn],
-                send_sem=x_send_sem.at[turn],
-                recv_sem=x_recv_sem.at[turn],
-                device_id=sibling,
-                device_id_type=MESH,
-            ).wait_recv()
+        if square and turn == 1:
+            for near, h in ((1, 0), (2, 1)):
+                pass_on(x_hbm, near, h, near).wait_recv()
+                onward = pass_on(pieces[near], 3, h, 3 - near)
+                onward.start()
+                sends.append(onward)
+        load(turn).wait()
+        for h in (0, 1) if turn else ():
+            if not (square and h == turn - 1):
+                pass_on(x_hbm, turn, h, direct[0]).wait_recv()
 
         def some(g, total, j=j, piece=pieces[turn], blocks=vals[turn]):
             for u in range(batch):
@@ -360,7 +372,7 @@
             pltpu.VMEM((line, unit + PAD, width), jnp.int16),
             pltpu.VMEM((line, unit + PAD, width), jnp.int16),
             pltpu.VMEM((line, unit + PAD, width), jnp.int16),
-            dma((n_blk,)), dma((n_blk,)), dma((n_blk,)),
+            dma((n_blk,)), dma((n_blk, 2)), dma((n_blk, 2)),
             dma((line,)), dma((line,)),
             dma((line, group)), dma((line, group)), dma((line, group)),
             dma, dma((5,)),

time: 26.6 us -> 26.4 us (level)
  no operation moved by 1% of the time
where the time goes in v4:
time: 26.4 us; the launch traced here: 26.3 us
  Pallas kernels  24.7 us (94%)
  local copies, waits for them, and re-layouts  1.62 us (6%)
    pallas_call x1, Pallas kernels, local(): pl.pallas_call(functools.partial(kernel, n_blk, line, group), out_shape=j...  24.7 us
    unnamed x1, local copies, waits for them, and re-layouts  1.62 us

profile of v4, /device:TPU:0, one launch (start us, length us, event | category | flops | bytes accessed | tf_op | source)
XLA Modules:
  0.0 26.3 jit_solution(8641095758590459484)
XLA Ops:
  0.0 24.7 %shard_map.64 = bf16[384,256]{1,0:T(8,128)(2,1)} custom-call(bf16[3,128,128]{2,1,0:T(8,128)(2,1)} %bitcast.6, bf16[4,40,128,128]{3,2,1,0:T(8,128)(2,1)} %bitcast.5, s32[4,40]{1,0:T(4,128)} %bitcast.7, s32[4,40]{1,0:T(4,128)} %bitcast.8, s32[1,4]{1,0:T(1,128)} %bitcast.9, bf16[128,256]{1,0:T(8,128)(2,1)} %w_hbm.1), custom_call_target="tpu_custom_call" | custom-call | flops 671088640 | bytes 5242880 | tf_op jit(solution)/shard_map/pallas_call | solution.py:356
  24.7 1.6 %copy.8 = bf16[384,256]{1,0:T(8,128)(2,1)} copy(bf16[384,256]{1,0:T(8,128)(2,1)} %shard_map.64) | data formatting | bytes 393216

commit v5 on v4

--- a/solution.py
+++ b/solution.py
@@ -44,8 +44,8 @@
     return part * (1.0 / LEVELS) * scale
 
 
-def prepare(rows_ref, cols_ref, count_ref, prep, panel, group):
-    lists, slots = rows_ref.shape
+def prepare(rows, cols, live_count, prep, base, nothing, panel, group):
+    slots = rows.shape[1]
     lane = lax.broadcasted_iota(jnp.int32, (slots, slots), 1)
     sub = lax.broadcasted_iota(jnp.int32, (slots, slots), 0)
     place = lax.broadcasted_iota(jnp.int32, (slots, panel), 1)
@@ -53,23 +53,22 @@
     slot_bits = max(1, (slots - 1).bit_length())
     row_bits = col_bits + slot_bits
 
-    for j in range(lists):
-        live = lane[0:1] < count_ref[0:1, j:j + 1]
-        key = jnp.where(live, rows_ref[j:j + 1, :], panel)
-        col = jnp.where(live, cols_ref[j:j + 1, :], 0)
-        word = key * (1 << row_bits) + lane[0:1] * (1 << col_bits) + col
-        spread = jnp.broadcast_to(word, (slots, slots))
-        word_up = jnp.sum(jnp.where(lane == sub, spread, 0), axis=1, keepdims=True)
-        rank = jnp.sum(jnp.where(word < word_up, 1, 0), axis=1, keepdims=True)
-        key_up = word_up >> row_bits
-        before = jnp.max(jnp.where(rank == lane - 1, key_up, -1), axis=0, keepdims=True)
-        ordered = jnp.sum(jnp.where(rank == lane, word_up, 0), axis=0, keepdims=True)
-        prep[j, 0:1, 0:slots] = (ordered >> col_bits) & ((1 << slot_bits) - 1)
-        prep[j, 1:2, 0:slots] = ordered & ((1 << col_bits) - 1)
-        prep[j, 2:3, 0:slots] = jnp.where(before == (ordered >> row_bits), 1, 0)
-        upto = jnp.sum(jnp.where(key_up <= place, 1, 0), axis=0, keepdims=True)
-        found = jnp.max(jnp.where(key_up == place, 1, 0), axis=0, keepdims=True)
-        prep[j, 3:4, 0:panel] = jnp.where(found > 0, upto + (j * slots - 1), lists * slots)
+    live = lane[0:1] < live_count
+    key = jnp.where(live, rows, panel)
+    col = jnp.where(live, cols, 0)
+    word = key * (1 << row_bits) + lane[0:1] * (1 << col_bits) + col
+    spread = jnp.broadcast_to(word, (slots, slots))
+    word_up = jnp.sum(jnp.where(lane == sub, spread, 0), axis=1, keepdims=True)
+    rank = jnp.sum(jnp.where(word < word_up, 1, 0), axis=1, keepdims=True)
+    key_up = word_up >> row_bits
+    before = jnp.max(jnp.where(rank == lane - 1, key_up, -1), axis=0, keepdims=True)
+    ordered = jnp.sum(jnp.where(rank == lane, word_up, 0), axis=0, keepdims=True)
+    prep[0:1, 0:slots] = (ordered >> col_bits) & ((1 << slot_bits) - 1)
+    prep[1:2, 0:slots] = ordered & ((1 << col_bits) - 1)
+    prep[2:3, 0:slots] = jnp.where(before == (ordered >> row_bits), 1, 0)
+    upto = jnp.sum(jnp.where(key_up <= place, 1, 0), axis=0, keepdims=True)
+    found = jnp.max(jnp.where(key_up == place, 1, 0), axis=0, keepdims=True)
+    prep[3:4, 0:panel] = jnp.where(found > 0, upto + (base - 1), nothing)
 
 
 def kernel(
@@ -155,17 +154,27 @@
     prep[...] = jnp.zeros(prep.shape, jnp.int32)
     for fetch in fetches[:3]:
         fetch.wait()
-    prepare(rows_ref, cols_ref, count_ref, prep, group * 2 * line, group)
-    fill = pltpu.make_async_copy(prep, table, table_sem)
-    fill.start()
+
+    def index(turn):
+        j = flip(blk, back(turn, n_blk), n_blk)
+        prepare(
+            rows_ref[pl.ds(j, 1), :], cols_ref[pl.ds(j, 1), :], count_ref[0, j],
+            prep.at[turn], turn * slots, n_blk * slots, group * 2 * line, group,
+        )
+
+    fills = [
+        pltpu.make_async_copy(prep.at[turn], table.at[turn], table_sem.at[turn])
+        for turn in range(n_blk)
+    ]
+    index(0)
+    fills[0].start()
     chain[n_blk * slots] = jnp.zeros((BS, width), jnp.float32)
 
-    fill.wait()
+    fills[0].wait()
     for fetch in fetches[3:]:
         fetch.wait()
-    batch = max(u for u in range(1, 21) if slots % u == 0)
+    batch = max(u for u in range(1, 41) if slots % u == 0)
     for turn in range(n_blk):
-        j = flip(blk, back(turn, n_blk), n_blk)
         if square and turn == 1:
             for near, h in ((1, 0), (2, 1)):
                 pass_on(x_hbm, near, h, near).wait_recv()
@@ -177,7 +186,10 @@
             if not (square and h == turn - 1):
                 pass_on(x_hbm, turn, h, direct[0]).wait_recv()
 
-        def some(g, total, j=j, piece=pieces[turn], blocks=vals[turn]):
+        if turn:
+            fills[turn].wait()
+
+        def some(g, total, j=turn, piece=pieces[turn], blocks=vals[turn]):
             for u in range(batch):
                 t = g * batch + u
                 product = jnp.dot(
@@ -189,7 +201,17 @@
                 chain[j * slots + t] = total
             return total
 
-        lax.fori_loop(0, slots // batch, some, jnp.zeros((BS, width), jnp.float32))
+        if turn == 0:
+            for later in range(1, n_blk):
+                index(later)
+        total = jnp.zeros((BS, width), jnp.float32)
+        if slots == batch:
+            some(0, total)
+        else:
+            lax.fori_loop(0, slots // batch, some, total)
+        if turn == 0:
+            for later in range(1, n_blk):
+                fills[later].start()
 
     def block_sum(k):
         total = chain[table[0, 3, k]]
@@ -361,7 +383,7 @@
         scratch_shapes=[
             pltpu.VMEM(rows.shape, jnp.int32),
             pltpu.VMEM(cols.shape, jnp.int32),
-            pltpu.VMEM(count.shape, jnp.int32),
+            pltpu.SMEM(count.shape, jnp.int32),
             pltpu.VMEM(weight.shape, jnp.bfloat16),
             pltpu.VMEM((n_blk, 8, 128), jnp.int32),
             pltpu.SMEM((n_blk, 8, 128), jnp.int32),
@@ -375,7 +397,7 @@
             dma((n_blk,)), dma((n_blk, 2)), dma((n_blk, 2)),
             dma((line,)), dma((line,)),
             dma((line, group)), dma((line, group)), dma((line, group)),
-            dma, dma((5,)),
+            dma((n_blk,)), dma((5,)),
         ]
         + [pltpu.VMEM((group, BS, width), jnp.bfloat16)] * n_blk
         + [pltpu.VMEM(vals.shape[1:], jnp.bfloat16)] * n_blk,

time: 26.4 us -> 26.3 us (level)
  no operation moved by 1% of the time
where the time goes in v5:
time: 26.3 us; the launch traced here: 26.2 us
  Pallas kernels  24.6 us (94%)
  local copies, waits for them, and re-layouts  1.62 us (6%)
    pallas_call x1, Pallas kernels, local(): pl.pallas_call(functools.partial(kernel, n_blk, line, group), out_shape=j...  24.6 us
    unnamed x1, local copies, waits for them, and re-layouts  1.62 us

profile of v5, /device:TPU:0, one launch (start us, length us, event | category | flops | bytes accessed | tf_op | source)
XLA Modules:
  0.0 26.2 jit_solution(18423888980580432982)
XLA Ops:
  0.0 24.6 %shard_map.64 = bf16[384,256]{1,0:T(8,128)(2,1)} custom-call(bf16[3,128,128]{2,1,0:T(8,128)(2,1)} %bitcast.6, bf16[4,40,128,128]{3,2,1,0:T(8,128)(2,1)} %bitcast.5, s32[4,40]{1,0:T(4,128)} %bitcast.7, s32[4,40]{1,0:T(4,128)} %bitcast.8, s32[1,4]{1,0:T(1,128)} %bitcast.9, bf16[128,256]{1,0:T(8,128)(2,1)} %w_hbm.1), custom_call_target="tpu_custom_call" | custom-call | flops 671088640 | bytes 5242880 | tf_op jit(solution)/shard_map/pallas_call | solution.py:378
  24.6 1.6 %copy.8 = bf16[384,256]{1,0:T(8,128)(2,1)} copy(bf16[384,256]{1,0:T(8,128)(2,1)} %shard_map.64) | data formatting | bytes 393216

commit v6 on v5

--- a/solution.py
+++ b/solution.py
@@ -1,4 +1,5 @@
 import functools
+import math
 
 import jax
 import jax.numpy as jnp
@@ -174,7 +175,27 @@
     for fetch in fetches[3:]:
         fetch.wait()
     batch = max(u for u in range(1, 41) if slots % u == 0)
+    lower = place < line // 2
+
+    def early_sum(k):
+        total = chain[table[0, 3, k]]
+        for turn in range(1, n_blk - 1):
+            total = total + chain[table[turn, 3, k]]
+        return total
+
+    def last_sum(k):
+        return chain[table[n_blk - 1, 3, k]]
+
+    def early(d, carry):
+        for g in range(group):
+            at = (d, pl.ds(g * BS, BS))
+            sib_send[at] = early_sum((2 * d + 1 - core) * group + g)
+            own[at] = early_sum((2 * d + core) * group + g)
+        return carry
+
     for turn in range(n_blk):
+        if turn == n_blk - 1:
+            lax.fori_loop(0, line, early, 0)
         if square and turn == 1:
             for near, h in ((1, 0), (2, 1)):
                 pass_on(x_hbm, near, h, near).wait_recv()
@@ -213,12 +234,6 @@
             for later in range(1, n_blk):
                 fills[later].start()
 
-    def block_sum(k):
-        total = chain[table[0, 3, k]]
-        for j in range(1, n_blk):
-            total = total + chain[table[j, 3, k]]
-        return total
-
     def sib_copy(d):
         return pltpu.make_async_remote_copy(
             src_ref=sib_send.at[d],
@@ -229,15 +244,15 @@
             device_id_type=MESH,
         )
 
-    lower = place < line // 2
-
     def gather(i, carry):
         d = jnp.where(lower, line - 1 - i, i)
         for g in range(group):
-            sib_send[d, g * BS:(g + 1) * BS] = block_sum((2 * d + 1 - core) * group + g)
+            at = (d, pl.ds(g * BS, BS))
+            sib_send[at] = sib_send[at] + last_sum((2 * d + 1 - core) * group + g)
         sib_copy(d).start()
         for g in range(group):
-            own[d, g * BS:(g + 1) * BS] = block_sum((2 * d + core) * group + g)
+            at = (d, pl.ds(g * BS, BS))
+            own[at] = own[at] + last_sum((2 * d + core) * group + g)
         return carry
 
     lax.fori_loop(0, line, gather, 0)
@@ -373,43 +388,51 @@
     slots = rows.shape[1]
     unit = group * BS
     vmem = pl.BlockSpec(memory_space=pltpu.VMEM)
-    anywhere = pl.BlockSpec(memory_space=pl.ANY)
+    far = pl.BlockSpec(memory_space=pltpu.HBM)
+    operands = (x, vals, rows, cols, count, weight)
     dma = pltpu.SemaphoreType.DMA
+    scratch = [
+        pltpu.VMEM(rows.shape, jnp.int32),
+        pltpu.VMEM(cols.shape, jnp.int32),
+        pltpu.SMEM(count.shape, jnp.int32),
+        pltpu.VMEM(weight.shape, jnp.bfloat16),
+        pltpu.VMEM((n_blk, 8, 128), jnp.int32),
+        pltpu.SMEM((n_blk, 8, 128), jnp.int32),
+        pltpu.VMEM((n_blk * slots + 1, BS, width), jnp.float32),
+        pltpu.VMEM((line, unit, width), jnp.float32),
+        pltpu.VMEM((line, unit, width), jnp.float32),
+        pltpu.VMEM((line, unit, width), jnp.float32),
+        pltpu.VMEM((line, unit + PAD, width), jnp.int16),
+        pltpu.VMEM((line, unit + PAD, width), jnp.int16),
+        pltpu.VMEM((line, unit + PAD, width), jnp.int16),
+    ]
+    semaphores = [
+        dma((n_blk,)), dma((n_blk, 2)), dma((n_blk, 2)),
+        dma((line,)), dma((line,)),
+        dma((line, group)), dma((line, group)), dma((line, group)),
+        dma((n_blk,)), dma((5,)),
+    ]
+    landing = [pltpu.VMEM((group, BS, width), jnp.bfloat16)] * n_blk
+    landing += [pltpu.VMEM(vals.shape[1:], jnp.bfloat16)] * n_blk
+    used = sum(
+        math.prod(ref.shape) * jnp.dtype(ref.dtype).itemsize
+        for ref in scratch + landing
+    )
     return pl.pallas_call(
         functools.partial(kernel, n_blk, line, group),
         out_shape=jax.ShapeDtypeStruct((unit, weight.shape[1]), jnp.bfloat16),
-        in_specs=[anywhere] * 6,
+        in_specs=[far] * 6,
         out_specs=vmem,
-        scratch_shapes=[
-            pltpu.VMEM(rows.shape, jnp.int32),
-            pltpu.VMEM(cols.shape, jnp.int32),
-            pltpu.SMEM(count.shape, jnp.int32),
-            pltpu.VMEM(weight.shape, jnp.bfloat16),
-            pltpu.VMEM((n_blk, 8, 128), jnp.int32),
-            pltpu.SMEM((n_blk, 8, 128), jnp.int32),
-            pltpu.VMEM((n_blk * slots + 1, BS, width), jnp.float32),
-            pltpu.VMEM((line, unit, width), jnp.float32),
-            pltpu.VMEM((line, unit, width), jnp.float32),
-            pltpu.VMEM((line, unit, width), jnp.float32),
-            pltpu.VMEM((line, unit + PAD, width), jnp.int16),
-            pltpu.VMEM((line, unit + PAD, width), jnp.int16),
-            pltpu.VMEM((line, unit + PAD, width), jnp.int16),
-            dma((n_blk,)), dma((n_blk, 2)), dma((n_blk, 2)),
-            dma((line,)), dma((line,)),
-            dma((line, group)), dma((line, group)), dma((line, group)),
-            dma((n_blk,)), dma((5,)),
-        ]
-        + [pltpu.VMEM((group, BS, width), jnp.bfloat16)] * n_blk
-        + [pltpu.VMEM(vals.shape[1:], jnp.bfloat16)] * n_blk,
+        scratch_shapes=scratch + semaphores + landing,
         compiler_params=pltpu.CompilerParams(
-            collective_id=0, has_side_effects=True, vmem_limit_bytes=56 * 1024 * 1024
+            collective_id=0, has_side_effects=True, vmem_limit_bytes=used + 4 * 1024 * 1024
         ),
         cost_estimate=pl.CostEstimate(
             flops=2 * n_blk * slots * BS * BS * width,
             bytes_accessed=2 * n_blk * slots * BS * BS,
             transcendentals=0,
         ),
-    )(x, vals, rows, cols, count, weight)
+    )(*(pltpu.with_memory_space_constraint(a, pltpu.HBM) for a in operands))
 
 
 def solution(mesh):

time: 26.3 us -> 24.7 us (0.939)
  local copies, waits for them, and re-layouts: 1.62 us -> 0.68 us
  Pallas kernels: 24.6 us -> 23.8 us
    unnamed x1, local copies, waits for them, and re-layouts: 1.62 us -> 0.68 us
    pallas_call x1, Pallas kernels: 24.6 us -> 23.8 us  [local(): pl.pallas_call(functools.partial(kernel, n_blk, line, group), out_shape=j...]
where the time goes in v6:
time: 24.7 us; the launch traced here: 24.5 us
  Pallas kernels  23.8 us (96%)
  local copies, waits for them, and re-layouts  0.68 us (3%)
    pallas_call x1, Pallas kernels, local(): pl.pallas_call(functools.partial(kernel, n_blk, line, group), out_shape=j...  23.8 us
    unnamed x1, local copies, waits for them, and re-layouts  0.68 us

profile of v6, /device:TPU:0, one launch (start us, length us, event | category | flops | bytes accessed | tf_op | source)
XLA Modules:
  0.0 24.5 jit_solution(12768280907921252733)
XLA Ops:
  0.0 23.8 %shard_map.64 = bf16[384,256]{1,0:T(8,128)(2,1)S(1)} custom-call(bf16[3,128,128]{2,1,0:T(8,128)(2,1)} %bitcast.6, bf16[4,40,128,128]{3,2,1,0:T(8,128)(2,1)} %bitcast.5, s32[4,40]{1,0:T(4,128)} %bitcast.7, s32[4,40]{1,0:T(4,128)} %bitcast.8, s32[1,4]{1,0:T(1,128)} %bitcast.9, bf16[128,256]{1,0:T(8,128)(2,1)} %w_hbm.1), custom_call_target="tpu_custom_call" | custom-call | flops 671088640 | bytes 5242880 | tf_op jit(solution)/shard_map/pallas_call | solution.py:421
  23.8 0.7 %copy.8 = bf16[384,256]{1,0:T(8,128)(2,1)} copy(bf16[384,256]{1,0:T(8,128)(2,1)S(1)} %shard_map.64) | data formatting | bytes 393216

commit v7 on v6

--- a/solution.py
+++ b/solution.py
@@ -244,15 +244,26 @@
             device_id_type=MESH,
         )
 
+    def order(i):
+        return jnp.where(lower, line - 1 - i, i)
+
     def gather(i, carry):
-        d = jnp.where(lower, line - 1 - i, i)
+        d = order(i)
         for g in range(group):
             at = (d, pl.ds(g * BS, BS))
             sib_send[at] = sib_send[at] + last_sum((2 * d + 1 - core) * group + g)
-        sib_copy(d).start()
+
+        @pl.when(i == 0)
+        def _():
+            sib_copy(d).start()
+
         for g in range(group):
             at = (d, pl.ds(g * BS, BS))
             own[at] = own[at] + last_sum((2 * d + core) * group + g)
+        return carry
+
+    def cross(i, carry):
+        sib_copy(order(i)).start()
         return carry
 
     lax.fori_loop(0, line, gather, 0)
@@ -326,7 +337,10 @@
 
         return carry
 
-    lax.fori_loop(0, line - 1, step, 0)
+    if line > 1:
+        step(0, 0)
+    lax.fori_loop(1, line, cross, 0)
+    lax.fori_loop(1, line - 1, step, 0)
 
     sib_copy(place).wait_recv()
     own[place] = own[place] + sib_recv[place]

time: 24.7 us -> 24.7 us (level)
  no operation moved by 1% of the time
where the time goes in v7:
time: 24.7 us; the launch traced here: 24.5 us
  Pallas kernels  23.8 us (96%)
  local copies, waits for them, and re-layouts  0.68 us (3%)
    pallas_call x1, Pallas kernels, local(): pl.pallas_call(functools.partial(kernel, n_blk, line, group), out_shape=j...  23.8 us
    unnamed x1, local copies, waits for them, and re-layouts  0.68 us

profile of v7, /device:TPU:0, one launch (start us, length us, event | category | flops | bytes accessed | tf_op | source)
XLA Modules:
  0.0 24.5 jit_solution(7282467466976074621)
XLA Ops:
  0.0 23.8 %shard_map.64 = bf16[384,256]{1,0:T(8,128)(2,1)S(1)} custom-call(bf16[3,128,128]{2,1,0:T(8,128)(2,1)} %bitcast.6, bf16[4,40,128,128]{3,2,1,0:T(8,128)(2,1)} %bitcast.5, s32[4,40]{1,0:T(4,128)} %bitcast.7, s32[4,40]{1,0:T(4,128)} %bitcast.8, s32[1,4]{1,0:T(1,128)} %bitcast.9, bf16[128,256]{1,0:T(8,128)(2,1)} %w_hbm.1), custom_call_target="tpu_custom_call" | custom-call | flops 671088640 | bytes 5242880 | tf_op jit(solution)/shard_map/pallas_call | solution.py:435
  23.8 0.7 %copy.8 = bf16[384,256]{1,0:T(8,128)(2,1)} copy(bf16[384,256]{1,0:T(8,128)(2,1)S(1)} %shard_map.64) | data formatting | bytes 393216

commit v8 on v6

--- a/solution.py
+++ b/solution.py
@@ -174,7 +174,7 @@
     fills[0].wait()
     for fetch in fetches[3:]:
         fetch.wait()
-    batch = max(u for u in range(1, 41) if slots % u == 0)
+    batch = max(u for u in range(2, 41, 2) if slots % u == 0)
     lower = place < line // 2
 
     def early_sum(k):
@@ -211,15 +211,26 @@
             fills[turn].wait()
 
         def some(g, total, j=turn, piece=pieces[turn], blocks=vals[turn]):
-            for u in range(batch):
+            for u in range(0, batch, 2):
                 t = g * batch + u
-                product = jnp.dot(
-                    blocks[table[j, 0, t]],
-                    piece[table[j, 1, t]],
+                left = [blocks[table[j, 0, t + v]] for v in (0, 1)]
+                right = [piece[table[j, 1, t + v]] for v in (0, 1)]
+                none = jnp.zeros_like(right[0])
+                both = jnp.dot(
+                    jnp.concatenate(left, axis=1),
+                    jnp.concatenate(
+                        [
+                            jnp.concatenate([right[0], none], axis=1),
+                            jnp.concatenate([none, right[1]], axis=1),
+                        ],
+                        axis=0,
+                    ),
                     preferred_element_type=jnp.float32,
                 )
-                total = total * table[j, 2, t].astype(jnp.float32) + product
-                chain[j * slots + t] = total
+                for v in (0, 1):
+                    product = both[:, v * width:(v + 1) * width]
+                    total = total * table[j, 2, t + v].astype(jnp.float32) + product
+                    chain[j * slots + t + v] = total
             return total
 
         if turn == 0:

time: 24.7 us -> 24.7 us (level)
  no operation moved by 1% of the time
where the time goes in v8:
time: 24.7 us; the launch traced here: 24.5 us
  Pallas kernels  23.8 us (96%)
  local copies, waits for them, and re-layouts  0.68 us (3%)
    pallas_call x1, Pallas kernels, local(): pl.pallas_call(functools.partial(kernel, n_blk, line, group), out_shape=j...  23.8 us
    unnamed x1, local copies, waits for them, and re-layouts  0.68 us

profile of v8, /device:TPU:0, one launch (start us, length us, event | category | flops | bytes accessed | tf_op | source)
XLA Modules:
  0.0 24.5 jit_solution(13180084304531460154)
XLA Ops:
  0.0 23.8 %shard_map.64 = bf16[384,256]{1,0:T(8,128)(2,1)S(1)} custom-call(bf16[3,128,128]{2,1,0:T(8,128)(2,1)} %bitcast.6, bf16[4,40,128,128]{3,2,1,0:T(8,128)(2,1)} %bitcast.5, s32[4,40]{1,0:T(4,128)} %bitcast.7, s32[4,40]{1,0:T(4,128)} %bitcast.8, s32[1,4]{1,0:T(1,128)} %bitcast.9, bf16[128,256]{1,0:T(8,128)(2,1)} %w_hbm.1), custom_call_target="tpu_custom_call" | custom-call | flops 671088640 | bytes 5242880 | tf_op jit(solution)/shard_map/pallas_call | solution.py:432
  23.9 0.7 %copy.8 = bf16[384,256]{1,0:T(8,128)(2,1)} copy(bf16[384,256]{1,0:T(8,128)(2,1)S(1)} %shard_map.64) | data formatting | bytes 393216
